TPU v7x, 32 devices: a whole 2x2x4 slice. The times are simulated.
32 devices in a mesh: lat: 4 (over y, x), lon: 8 (over z, core).
Axes of the slice: x: 2, y: 2, z: 4, core: 2. Of those that a mesh axis runs over, the one named last changes fastest.
Arguments:
- fields_in: bfloat16 [8, 256, 1024], P(None, 'lat', 'lon'), may hold values from -6 to 6
- hidden: bfloat16 [64, 256, 1024], P(None, 'lat', 'lon'), may hold values from -2.5 to 2.5
- cell_state: float32 [64, 256, 1024], P(None, 'lat', 'lon'), may hold values from -6 to 6
- analysis: bfloat16 [8, 256, 1024], P(None, 'lat', 'lon'), may hold values from -6 to 6, as said below
- gate_weight: bfloat16 [256, 648], replicated, may hold values from -0.25 to 0.25
- gate_bias: float32 [256], replicated, may hold values from -4 to 4
- out_weight: bfloat16 [8, 64], replicated, may hold values from -0.75 to 0.75
- relax_rates: float32 [8, 214], replicated, may hold values from 0.05 to 1
Outputs:
- fields_out: bfloat16 [8, 256, 1024], P(None, 'lat', 'lon')
- hidden_out: bfloat16 [64, 256, 1024], P(None, 'lat', 'lon')
- cell_out: float32 [64, 256, 1024], P(None, 'lat', 'lon')
Inputs may be any that keep to these rules, and one draw needn't show every extreme that they name: analysis fields of order one.
All inputs are finite; a program needn't handle non-finite values.
Results may differ from a plain program's by a relative error of at most 0.009.
Values may be sent and summed in bfloat16 or wider, within the bound.
A program may use at most 448 MiB of HBM per device.

v0:
```python
import functools
import math

import jax
import jax.numpy as jnp
import numpy as np
from jax import lax
from jax.experimental import pallas as pl
from jax.experimental.pallas import tpu as pltpu
from jax.sharding import PartitionSpec as P

FIELDS = 8
TRUNC = 213
MODES = 224
KDEG = 214
CH = 80
QP = 16
KP = 256
MESH = pl.DeviceIdType.MESH
F32 = jnp.float32
BF16 = jnp.bfloat16


def legendre_table(lat_total, owners, share):
    order = np.arange(MODES) * 1.0
    ratios = np.ones(MODES)
    ratios[1:] = (2.0 * order[1:] + 1.0) / (2.0 * order[1:])
    diag_log = 0.5 * np.log(0.5) + np.cumsum(0.5 * np.log(ratios))
    phi = -0.5 * np.pi + (np.arange(lat_total) + 0.5) * np.pi / lat_total
    sine, cosine = np.sin(phi), np.cos(phi)
    table = np.zeros((KDEG, MODES, lat_total))
    table[0] = np.exp(diag_log[:, None] + order[:, None] * np.log(cosine)[None, :])
    table[1] = np.sqrt(2.0 * order + 3.0)[:, None] * sine[None, :] * table[0]
    for k in range(2, KDEG):
        n = order + k
        alpha = np.sqrt((4.0 * n**2 - 1.0) / (n**2 - order**2))
        beta = np.sqrt(((n - 1.0) ** 2 - order**2) / (4.0 * (n - 1.0) ** 2 - 1.0))
        table[k] = alpha[:, None] * (sine[None, :] * table[k - 1] - beta[:, None] * table[k - 2])
    degree = order[None, :] + np.arange(KDEG)[:, None]
    table *= (degree <= TRUNC)[:, :, None]
    full = np.zeros((owners * share, KP, lat_total), dtype=BF16)
    full[:MODES, :KDEG] = table.transpose(1, 0, 2).astype(np.float32).astype(BF16)
    return full.reshape(owners, share * KP, lat_total)


def trig_table(lon_total, owners, share):
    m = np.arange(owners * share)
    phase = (m[:, None] * np.arange(lon_total)[None, :]) % lon_total
    angle = phase * (2.0 * np.pi / lon_total)
    both = np.stack([np.cos(angle), np.sin(angle)], axis=1) * (m <= TRUNC)[:, None, None]
    full = np.zeros((owners, QP, lon_total))
    full[:, : 2 * share] = both.reshape(owners, 2 * share, lon_total)
    return full.reshape(owners * QP, lon_total).astype(np.float32).astype(BF16)


def kernel(
    lats, lons, share, rows, cols,
    fields_ref, hidden_ref, cell_ref, analysis_ref, gw_ref, bias_ref, ow_ref, relax_ref,
    weights_ref, trig_hbm, leg_hbm,
    fields_out, hidden_out, cell_out,
    send1, r1, fh, slab, cols_out, halo, cols_in, fsend, r2, xbuf, ysend, r3, csend, r4,
    gate_w, pred, hid, trig, leg, cell,
    load_sem, s1, v1, s2, v2, s3, v3, s4, v4, sh, vh,
):
    a, b = lax.axis_index("lat"), lax.axis_index("lon")
    owners = lats * lons
    me = a * lons + b
    piece = FIELDS * rows // lons
    per_field = rows // piece
    packs = 128 // piece
    group = a * per_field + lax.rem(b, per_field)
    own_row = pl.multiple_of(lax.rem(group, packs) * piece, piece)
    lon_total = lons * cols

    load_trig = pltpu.make_async_copy(trig_hbm, trig, load_sem.at[0])
    load_leg = pltpu.make_async_copy(leg_hbm.at[me], leg, load_sem.at[1])
    load_cell = pltpu.make_async_copy(cell_ref, cell, load_sem.at[2])
    load_trig.start()
    load_leg.start()
    load_cell.start()

    r1[...] = jnp.zeros_like(r1)
    barrier = pltpu.get_barrier_semaphore()

    def greet(i, _):
        peer = lax.rem(me + i, owners)
        pl.semaphore_signal(
            barrier, inc=1, device_id=(peer // lons, lax.rem(peer, lons)), device_id_type=MESH
        )
        return 0

    lax.fori_loop(1, owners, greet, 0)

    send1[...] = (analysis_ref[...].astype(F32) - fields_ref[...].astype(F32)).astype(BF16)
    pl.semaphore_wait(barrier, owners - 1)

    def lon_copy(i, src, dst, ssem, rsem):
        return pltpu.make_async_remote_copy(
            src_ref=src, dst_ref=dst, send_sem=ssem.at[i], recv_sem=rsem.at[i],
            device_id=(a, lax.rem(b + i, lons)), device_id_type=MESH,
        )

    def first(i):
        peer = lax.rem(b + i, lons)
        src = send1.at[pl.ds(pl.multiple_of(peer * piece, piece), piece)]
        return lon_copy(i, src, r1.at[b, pl.ds(own_row, piece)], s1, v1)

    def loop(start, stop, fn):
        def body(i, _):
            fn(i)
            return 0
        lax.fori_loop(start, stop, body, 0)

    loop(1, lons, lambda i: first(i).start())
    r1[b, pl.ds(own_row, piece), :] = send1[pl.ds(pl.multiple_of(b * piece, piece), piece), :]

    fh[0 : FIELDS * rows, :] = fields_ref[...].astype(F32)

    def widen(c):
        at = pl.multiple_of(c * 512, 512)
        fh[pl.ds(pl.multiple_of(at + FIELDS * rows, 512), 512), :] = hidden_ref[
            pl.ds(at, 512), :
        ].astype(F32)

    loop(0, hidden_ref.shape[0] // 512, widen)
    lane = lax.broadcasted_iota(jnp.int32, (CH, cols), 1)
    ones = jnp.ones((8, cols), F32)

    def turn(r, carry):
        west, east = carry
        t = jnp.concatenate([fh[pl.ds(r, CH - 8, stride=rows), :], ones], axis=0)
        slab[r + 1, CH : 2 * CH, :] = t.astype(BF16)
        west = jnp.where(lane == r, jnp.broadcast_to(t[:, 0:1], (CH, cols)), west)
        east = jnp.where(lane == r, jnp.broadcast_to(t[:, cols - 1 : cols], (CH, cols)), east)
        return west, east

    zero = jnp.zeros((CH, cols), F32)
    west, east = lax.fori_loop(0, rows, turn, (zero, zero))
    cols_out[0] = west.astype(BF16)
    cols_out[1] = east.astype(BF16)

    left, right = lax.rem(b + lons - 1, lons), lax.rem(b + 1, lons)

    def rim(slot, src, dst, la, lo):
        return pltpu.make_async_remote_copy(
            src_ref=src, dst_ref=dst, send_sem=sh.at[slot], recv_sem=vh.at[slot],
            device_id=(la, lo), device_id_type=MESH,
        )

    north, south = jnp.maximum(a - 1, 0), jnp.minimum(a + 1, lats - 1)
    to_south = [
        rim(0, slab.at[rows, pl.ds(CH, CH)], halo.at[0], south, b),
        rim(1, cols_out.at[1], cols_in.at[0, 0], south, right),
        rim(2, cols_out.at[0], cols_in.at[1, 0], south, left),
    ]
    to_north = [
        rim(3, slab.at[1, pl.ds(CH, CH)], halo.at[1], north, b),
        rim(4, cols_out.at[1], cols_in.at[0, 2], north, right),
        rim(5, cols_out.at[0], cols_in.at[1, 2], north, left),
    ]
    level = [
        rim(6, cols_out.at[1], cols_in.at[0, 1], a, right),
        rim(7, cols_out.at[0], cols_in.at[1, 1], a, left),
    ]
    for copy in level:
        copy.start()

    @pl.when(a < lats - 1)
    def _():
        for copy in to_south:
            copy.start()

    @pl.when(a > 0)
    def _():
        for copy in to_north:
            copy.start()

    load_trig.wait()
    loop(1, lons, lambda i: first(i).wait())
    lat_weight = weights_ref[pl.ds(group // packs, 1), :]
    tall = min(512, owners * QP)

    def zonal(c):
        at = pl.multiple_of(c * tall, tall)
        total = jnp.zeros((tall, 128), F32)
        for x in range(lons):
            total += lax.dot_general(
                trig[pl.ds(at, tall), x * cols : (x + 1) * cols], r1[x],
                (((1,), (1,)), ((), ())), preferred_element_type=F32,
            )
        fsend[pl.ds(at, tall), :] = (total * lat_weight).astype(BF16)

    loop(0, owners * QP // tall, zonal)

    def own_block(ref, d):
        return ref.at[pl.ds(pl.multiple_of(d * QP, QP), QP)]

    def second(i):
        peer = lax.rem(me + i, owners)
        return pltpu.make_async_remote_copy(
            src_ref=own_block(fsend, peer), dst_ref=own_block(r2, me),
            send_sem=s2.at[i], recv_sem=v2.at[i],
            device_id=(peer // lons, lax.rem(peer, lons)), device_id_type=MESH,
        )

    loop(1, owners, lambda i: second(i).start())
    mine = pl.ds(pl.multiple_of(me * QP, QP), QP)
    r2[mine, :] = fsend[mine, :]

    wide = 9 * CH
    spot = lax.broadcasted_iota(jnp.int32, (1, wide), 1)
    tap = spot // CH
    within = spot - tap * CH
    source = jnp.where(within < CH - 8, tap * (CH - 8) + within, -1)
    pick = lax.broadcasted_iota(jnp.int32, (gw_ref.shape[1], wide), 0) == source
    spread = jnp.dot(
        gw_ref[...], jnp.where(pick, 1.0, 0.0).astype(BF16), preferred_element_type=F32
    )
    bias = jnp.transpose(jnp.broadcast_to(bias_ref[...], (128, 256)))[:, 0:1]
    high = bias.astype(BF16).astype(F32)
    middle = (bias - high).astype(BF16).astype(F32)
    low = bias - high - middle
    base = 4 * CH + CH - 8
    spread += jnp.where(spot == base, high, 0.0)
    spread += jnp.where(spot == base + 1, middle, 0.0)
    spread += jnp.where(spot == base + 2, low, 0.0)
    gate_row = lax.broadcasted_iota(jnp.int32, (256, 1), 0) // 64
    gate_w[...] = (spread * jnp.where(gate_row == 2, 1.0, 0.5)).astype(BF16)

    for copy in level:
        copy.wait()

    @pl.when(a < lats - 1)
    def _():
        for copy in to_south:
            copy.wait_send()
        for copy in to_north:
            copy.wait_recv()

    @pl.when(a > 0)
    def _():
        for copy in to_north:
            copy.wait_send()
        for copy in to_south:
            copy.wait_recv()

    @pl.when(a == 0)
    def _():
        halo[0] = jnp.zeros((CH, cols), BF16)
        cols_in[0, 0] = jnp.zeros((CH, cols), BF16)
        cols_in[1, 0] = jnp.zeros((CH, cols), BF16)

    @pl.when(a == lats - 1)
    def _():
        halo[1] = jnp.zeros((CH, cols), BF16)
        cols_in[0, 2] = jnp.zeros((CH, cols), BF16)
        cols_in[1, 2] = jnp.zeros((CH, cols), BF16)

    def shifted(t, from_west, from_east, row, at):
        before = jnp.where(lane == 0, pltpu.roll(from_west, lax.rem(cols - row, cols), 1), pltpu.roll(t, 1, 1))
        after = jnp.where(
            lane == cols - 1, pltpu.roll(from_east, cols - 1 - row, 1), pltpu.roll(t, cols - 1, 1)
        )
        slab[at, 0:CH, :] = before.astype(BF16)
        slab[at, 2 * CH : 3 * CH, :] = after.astype(BF16)

    def shift_row(r):
        t = slab[r + 1, CH : 2 * CH, :].astype(F32)
        shifted(t, cols_in[0, 1].astype(F32), cols_in[1, 1].astype(F32), r, r + 1)

    loop(0, rows, shift_row)
    slab[0, CH : 2 * CH, :] = halo[0]
    slab[rows + 1, CH : 2 * CH, :] = halo[1]
    shifted(halo[0].astype(F32), cols_in[0, 0].astype(F32), cols_in[1, 0].astype(F32), rows - 1, 0)
    shifted(halo[1].astype(F32), cols_in[0, 2].astype(F32), cols_in[1, 2].astype(F32), 0, rows + 1)

    load_leg.wait()
    loop(1, owners, lambda i: second(i).wait())
    tiles = lats * rows // 128
    for f in range(FIELDS):
        for t in range(tiles):
            total = jnp.zeros((QP, 128), F32)
            for s in range(packs):
                g = t * packs + s
                d = (g // per_field) * lons + f * per_field + g % per_field
                total += r2[d * QP : (d + 1) * QP, :].astype(F32)
            xbuf[f * QP : (f + 1) * QP, t * 128 : (t + 1) * 128] = total.astype(BF16)
    x = xbuf[...]
    y = jnp.zeros((FIELDS * QP, lats * rows), F32)
    q_mode = lax.rem(lax.broadcasted_iota(jnp.int32, (FIELDS * QP, KP), 0), QP) // 2
    m_first = me * share
    rates = pltpu.roll(relax_ref[...], lax.rem(512 - m_first, 512), 1)
    for i in range(share):
        basis = leg[i * KP : (i + 1) * KP, :]
        s = lax.dot_general(x, basis, (((1,), (1,)), ((), ())), preferred_element_type=F32)
        rate = (rates if i == 0 else pltpu.roll(rates, 512 - i, 1))[:, :KP]
        rate = rate * jnp.where(m_first + i == 0, 1.0 / lon_total, 2.0 / lon_total)
        rate = jnp.broadcast_to(rate[:, None, :], (FIELDS, QP, KP)).reshape(FIELDS * QP, KP)
        s = jnp.where(q_mode == i, s * rate, 0.0).astype(BF16)
        y += jnp.dot(s, basis, preferred_element_type=F32)
    y = y.astype(BF16)
    for t in range(tiles):
        ysend[t] = y[:, t * 128 : (t + 1) * 128]

    def reply(d):
        la, lo = d // lons, lax.rem(d, lons)
        t = (la * per_field + lax.rem(lo, per_field)) // packs
        return t, pl.ds(pl.multiple_of((lo // per_field) * QP, QP), QP)

    def third(i):
        peer = lax.rem(me + i, owners)
        t, at = reply(peer)
        return pltpu.make_async_remote_copy(
            src_ref=ysend.at[t, at], dst_ref=own_block(r3, me),
            send_sem=s3.at[i], recv_sem=v3.at[i],
            device_id=(peer // lons, lax.rem(peer, lons)), device_id_type=MESH,
        )

    loop(1, owners, lambda i: third(i).start())
    t_own, at_own = reply(me)
    r3[mine, :] = ysend[t_own, at_own, :]

    load_cell.wait()

    def pair(i):
        r = 2 * i
        patches = jnp.concatenate(
            [slab[pl.ds(r, 3)].reshape(wide, cols), slab[pl.ds(r + 1, 3)].reshape(wide, cols)], axis=1
        )
        g = jnp.tanh(jnp.dot(gate_w[...], patches, preferred_element_type=F32))
        old = jnp.concatenate(
            [cell[pl.ds(r, 64, stride=rows), :], cell[pl.ds(r + 1, 64, stride=rows), :]], axis=1
        )
        new = (0.5 * g[64:128] + 0.5) * old + (0.5 * g[0:64] + 0.5) * g[128:192]
        h = (0.5 * g[192:256] + 0.5) * jnp.tanh(new)
        cell_out[pl.ds(r, 64, stride=rows), :] = new[:, :cols]
        cell_out[pl.ds(r + 1, 64, stride=rows), :] = new[:, cols:]
        hid[pl.ds(r, 64, stride=rows), :] = h[:, :cols]
        hid[pl.ds(r + 1, 64, stride=rows), :] = h[:, cols:]
        inc = jnp.dot(ow_ref[...], h.astype(BF16), preferred_element_type=F32)
        pred[pl.ds(r, FIELDS, stride=rows), :] = inc[:, :cols]
        pred[pl.ds(r + 1, FIELDS, stride=rows), :] = inc[:, cols:]

    loop(0, rows // 4, pair)

    loop(1, owners, lambda i: third(i).wait())
    for c in range(lons):
        csend[c] = lax.dot_general(
            r3[...], trig[:, c * cols : (c + 1) * cols], (((0,), (0,)), ((), ())),
            preferred_element_type=F32,
        ).astype(BF16)
    spot4 = pl.ds(pl.multiple_of(b * piece, piece), piece)

    def fourth(i):
        peer = lax.rem(b + i, lons)
        return lon_copy(i, csend.at[peer, pl.ds(own_row, piece)], r4.at[spot4], s4, v4)

    loop(1, lons, lambda i: fourth(i).start())
    r4[spot4, :] = csend[b, pl.ds(own_row, piece), :]

    loop(rows // 4, rows // 2, pair)

    def narrow(c):
        at = pl.ds(pl.multiple_of(c * 512, 512), 512)
        hidden_out[at, :] = hid[at, :].astype(BF16)

    loop(0, hidden_ref.shape[0] // 512, narrow)
    loop(1, lons, lambda i: fourth(i).wait())
    fields_out[...] = (
        fields_ref[...].astype(F32) + pred[...] + r4[...].astype(F32)
    ).astype(BF16)


def local(lats, lons, leg, trig, share, fields_in, hidden, cell_state, analysis, gate_weight, gate_bias, out_weight, relax_rates):
    hid, rows, cols = cell_state.shape
    owners = lats * lons
    lat_total = lats * rows
    piece = FIELDS * rows // lons
    phi = -0.5 * np.pi + (np.arange(lat_total) + 0.5) * np.pi / lat_total
    weights = (np.cos(phi) * np.pi / lat_total).astype(np.float32).reshape(-1, 128)
    vm = pl.BlockSpec(memory_space=pltpu.VMEM)
    hbm = pl.BlockSpec(memory_space=pl.ANY)
    n_rows = FIELDS * rows
    dma = pltpu.SemaphoreType.DMA
    relax = jnp.pad(relax_rates, ((0, 0), (0, 512 - KDEG)))
    out = pl.pallas_call(
        functools.partial(kernel, lats, lons, share, rows, cols),
        out_shape=(
            jax.ShapeDtypeStruct((n_rows, cols), BF16),
            jax.ShapeDtypeStruct((hid * rows, cols), BF16),
            jax.ShapeDtypeStruct((hid * rows, cols), F32),
        ),
        in_specs=[vm, vm, hbm, vm, vm, vm, vm, vm, vm, hbm, hbm],
        out_specs=(vm, vm, vm),
        scratch_shapes=[
            pltpu.VMEM((n_rows, cols), BF16),
            pltpu.VMEM((lons, 128, cols), BF16),
            pltpu.VMEM(((hid + FIELDS) * rows, cols), F32),
            pltpu.VMEM((rows + 2, 3 * CH, cols), BF16),
            pltpu.VMEM((2, CH, cols), BF16),
            pltpu.VMEM((2, CH, cols), BF16),
            pltpu.VMEM((2, 3, CH, cols), BF16),
            pltpu.VMEM((owners * QP, 128), BF16),
            pltpu.VMEM((owners * QP, 128), BF16),
            pltpu.VMEM((FIELDS * QP, lat_total), BF16),
            pltpu.VMEM((lat_total // 128, FIELDS * QP, 128), BF16),
            pltpu.VMEM((owners * QP, 128), BF16),
            pltpu.VMEM((lons, 128, cols), BF16),
            pltpu.VMEM((n_rows, cols), BF16),
            pltpu.VMEM((4 * hid, 9 * CH), BF16),
            pltpu.VMEM((n_rows, cols), F32),
            pltpu.VMEM((hid * rows, cols), F32),
            pltpu.VMEM(trig.shape, BF16),
            pltpu.VMEM(leg.shape[1:], BF16),
            pltpu.VMEM((hid * rows, cols), F32),
            dma((3,)),
            dma((lons,)), dma((lons,)), dma((owners,)), dma((owners,)),
            dma((owners,)), dma((owners,)), dma((lons,)), dma((lons,)),
            dma((8,)), dma((8,)),
        ],
        compiler_params=pltpu.CompilerParams(
            collective_id=0, has_side_effects=True, vmem_limit_bytes=56 * 1024 * 1024
        ),
    )(
        fields_in.reshape(n_rows, cols), hidden.reshape(hid * rows, cols),
        cell_state.reshape(hid * rows, cols), analysis.reshape(n_rows, cols),
        gate_weight, gate_bias.reshape(1, -1), out_weight, relax, jnp.asarray(weights),
        jnp.asarray(trig), jnp.asarray(leg),
    )
    return (
        out[0].reshape(fields_in.shape), out[1].reshape(hidden.shape), out[2].reshape(cell_state.shape)
    )


def solution(mesh):
    lats, lons = mesh.shape["lat"], mesh.shape["lon"]
    owners = lats * lons
    share = -(-MODES // owners)

    def whole(*args):
        lat_total, lon_total = args[2].shape[1:]
        leg = legendre_table(lat_total, owners, share)
        trig = trig_table(lon_total, owners, share)
        grid = P(None, "lat", "lon")
        return jax.shard_map(
            functools.partial(local, lats, lons, leg, trig, share),
            mesh=mesh,
            in_specs=(grid, grid, grid, grid, P(), P(), P(), P()),
            out_specs=(grid, grid, grid),
            check_vma=False,
        )(*args)

    return whole
```

profile of v0, /device:TPU:0, one launch (start us, length us, event | category | flops | bytes accessed | tf_op | source)
XLA Modules:
  0.0 57.9 jit_solution(9714876532508107375)
XLA Ops:
  0.6 1.3 %pad.4.relax_ref = f32[8,512]{1,0:T(8,128)} pad(f32[8,214]{1,0:T(8,128)} %param.18, f32[]{:T(128)} %constant.8.clone.1), padding=0_0x0_298 | pad | bytes 23236 | tf_op jit(solution)/shard_map/jit(_pad)/pad | solution.py:385
  1.9 1.9 %copy.14.gw_ref = bf16[256,648]{1,0:T(8,128)(2,1)} copy(bf16[256,648]{0,1:T(8,128)(2,1)} %param.15) | data formatting | bytes 663552 | tf_op args[4]
  3.8 48.8 %shard_map.130 = (bf16[512,128]{1,0:T(8,128)(2,1)}, bf16[4096,128]{1,0:T(8,128)(2,1)}, f32[4096,128]{1,0:T(8,128)}) custom-call(bf16[512,128]{1,0:T(8,128)(2,1)} %bitcast.12, bf16[4096,128]{1,0:T(8,128)(2,1)} %bitcast.10, f32[4096,128]{1,0:T(8,128)} %bitcast.8, bf16[512,128]{1,0:T(8,128)(2,1)} %bitcast.13, bf16[256,648]{1,0:T(8,128)(2,1)} %copy.14.gw_ref, ...), custom_call_target="tpu_custom_call" | custom-call | tf_op jit(solution)/shard_map/pallas_call | solution.py:386
  52.6 0.0 copy-start
  52.6 1.7 %copy.18 = bf16[8,64,128]{2,1,0:T(8,128)(2,1)} copy(bf16[8,64,128]{2,1,0:T(8,128)(2,1)} %bitcast.14) | data formatting | bytes 262144
  54.3 2.3 %copy.19 = bf16[64,64,128]{2,1,0:T(8,128)(2,1)} copy(bf16[64,64,128]{2,1,0:T(8,128)(2,1)} %bitcast.11) | data formatting | bytes 2097152
  56.6 0.0 copy-done
  56.6 1.3 %copy.20 = f32[64,64,128]{2,1,0:T(8,128)} copy(f32[64,64,128]{2,1,0:T(8,128)S(1)} %bitcast.9) | data formatting | bytes 4194304
Async XLA Ops:
  52.6 4.0 %copy-start = (f32[4096,128]{1,0:T(8,128)S(1)}, f32[4096,128]{1,0:T(8,128)}, u32[]{:S(2)}) copy-start(f32[4096,128]{1,0:T(8,128)} %get-tuple-element.8) | copy-start | bytes 6291460
where the time goes:
time: 58.2 us; the launch traced here: 57.9 us
  Pallas kernels  48.8 us (84%)
  local copies, waits for them, and re-layouts  8.5 us (15%)
  between operations  0.65 us (1%)
    pallas_call x1, Pallas kernels, local(): pl.pallas_call(functools.partial(kernel, lats, lons, share, rows, cols),...  48.8 us
    unnamed x6, local copies, waits for them, and re-layouts  7.19 us
    pad x1, local copies, waits for them, and re-layouts, local(): relax = jnp.pad(relax_rates, ((0, 0), (0, 512 - KDEG)))  1.31 us

commit v1 on v0

v1 whole, which is shorter than its diff:
```python
import functools
import math

import jax
import jax.numpy as jnp
import numpy as np
from jax import lax
from jax.experimental import pallas as pl
from jax.experimental.pallas import tpu as pltpu
from jax.sharding import PartitionSpec as P

FIELDS = 8
TRUNC = 213
MODES = 224
KDEG = 214
CH = 80
MESH = pl.DeviceIdType.MESH
F32 = jnp.float32
BF16 = jnp.bfloat16


def legendre_table(lat_total, members):
    order = np.arange(MODES) * 1.0
    ratios = np.ones(MODES)
    ratios[1:] = (2.0 * order[1:] + 1.0) / (2.0 * order[1:])
    diag_log = 0.5 * np.log(0.5) + np.cumsum(0.5 * np.log(ratios))
    phi = -0.5 * np.pi + (np.arange(lat_total) + 0.5) * np.pi / lat_total
    sine, cosine = np.sin(phi), np.cos(phi)
    table = np.zeros((KDEG, MODES, lat_total))
    table[0] = np.exp(diag_log[:, None] + order[:, None] * np.log(cosine)[None, :])
    table[1] = np.sqrt(2.0 * order + 3.0)[:, None] * sine[None, :] * table[0]
    for k in range(2, KDEG):
        n = order + k
        alpha = np.sqrt((4.0 * n**2 - 1.0) / (n**2 - order**2))
        beta = np.sqrt(((n - 1.0) ** 2 - order**2) / (4.0 * (n - 1.0) ** 2 - 1.0))
        table[k] = alpha[:, None] * (sine[None, :] * table[k - 1] - beta[:, None] * table[k - 2])
    degree = order[None, :] + np.arange(KDEG)[:, None]
    table *= (degree <= TRUNC)[:, :, None]
    offsets = degree_offsets(members)
    full = np.zeros((members, offsets[-1], lat_total))
    for member in range(members):
        for i, m in enumerate(range(member, MODES, members)):
            count = min(offsets[i + 1] - offsets[i], KDEG)
            full[member, offsets[i] : offsets[i] + count] = table[:count, m]
    return full.astype(np.float32).astype(BF16)


def degree_offsets(members):
    offsets = [0]
    for i in range(-(-MODES // members)):
        offsets.append(offsets[-1] + (256 if KDEG - members * i > 128 else 128))
    return offsets


def block_rows(members):
    return -(-2 * -(-MODES // members) // 16) * 16


def trig_table(lon_total, members):
    m = np.arange(-(-MODES // members) * members)
    phase = (m[:, None] * np.arange(lon_total)[None, :]) % lon_total
    angle = phase * (2.0 * np.pi / lon_total)
    both = np.stack([np.cos(angle), np.sin(angle)], axis=1) * (m <= TRUNC)[:, None, None]
    full = np.zeros((members, block_rows(members), lon_total))
    for member in range(members):
        part = both[member::members].reshape(-1, lon_total)
        full[member, : part.shape[0]] = part
    return full.reshape(-1, lon_total).astype(np.float32).astype(BF16)


def loop(start, stop, fn):
    def body(i, _):
        fn(i)
        return 0

    lax.fori_loop(start, stop, body, 0)


def kernel(
    lats, lons, rows, cols,
    fields_ref, hidden_ref, cell_ref, analysis_ref, gw_ref, bias_ref, ow_ref, relax_ref,
    weights_ref, trig_hbm, leg_hbm,
    fields_out, hidden_out, cell_out,
    send1, r1, fh, slab, cols_out, halo, cols_in, fsend, r2, ysend, r3, turned, csend, r4, rates,
    gate_w, pred, hid, trig, leg, cell,
    load_sem, s1, v1, s2, v2, s3, v3, s4, v4, sh, vh,
):
    a, b = lax.axis_index("lat"), lax.axis_index("lon")
    piece = FIELDS * rows // lons
    per_field = rows // piece
    packs = 128 // piece
    group = a * per_field + lax.rem(b, per_field)
    members = lats * per_field
    block = block_rows(members)
    own_row = pl.multiple_of(lax.rem(group, packs) * piece, piece)
    lon_total = lons * cols

    load_trig = pltpu.make_async_copy(trig_hbm, trig, load_sem.at[0])
    load_leg = pltpu.make_async_copy(leg_hbm.at[group], leg, load_sem.at[1])
    load_cell = pltpu.make_async_copy(cell_ref, cell, load_sem.at[2])
    load_trig.start()
    load_leg.start()
    load_cell.start()

    r1[...] = jnp.zeros_like(r1)
    barrier = pltpu.get_barrier_semaphore()

    def member_device(member):
        return member // per_field, b - lax.rem(b, per_field) + lax.rem(member, per_field)

    def hello(la, lo):
        pl.semaphore_signal(barrier, inc=1, device_id=(la, lo), device_id_type=MESH)

    loop(1, lons, lambda i: hello(a, lax.rem(b + i, lons)))
    loop(1, members, lambda i: hello(*member_device(lax.rem(group + i, members))))
    left, right = lax.rem(b + lons - 1, lons), lax.rem(b + 1, lons)
    north, south = jnp.maximum(a - 1, 0), jnp.minimum(a + 1, lats - 1)

    @pl.when(a > 0)
    def _():
        hello(north, left)
        hello(north, right)

    @pl.when(a < lats - 1)
    def _():
        hello(south, left)
        hello(south, right)

    send1[...] = (analysis_ref[...].astype(F32) - fields_ref[...].astype(F32)).astype(BF16)
    greeted = lons + members - 2
    greeted += 2 * (a > 0).astype(jnp.int32) + 2 * (a < lats - 1).astype(jnp.int32)
    pl.semaphore_wait(barrier, greeted)

    def lon_copy(i, src, dst, ssem, rsem):
        return pltpu.make_async_remote_copy(
            src_ref=src, dst_ref=dst, send_sem=ssem.at[i], recv_sem=rsem.at[i],
            device_id=(a, lax.rem(b + i, lons)), device_id_type=MESH,
        )

    def first(i):
        peer = lax.rem(b + i, lons)
        src = send1.at[pl.ds(pl.multiple_of(peer * piece, piece), piece)]
        return lon_copy(i, src, r1.at[b, pl.ds(own_row, piece)], s1, v1)

    loop(1, lons, lambda i: first(i).start())
    r1[b, pl.ds(own_row, piece), :] = send1[pl.ds(pl.multiple_of(b * piece, piece), piece), :]

    fh[0 : FIELDS * rows, :] = fields_ref[...].astype(F32)

    def widen(c):
        at = pl.multiple_of(c * 512, 512)
        fh[pl.ds(pl.multiple_of(at + FIELDS * rows, 512), 512), :] = hidden_ref[
            pl.ds(at, 512), :
        ].astype(F32)

    loop(0, hidden_ref.shape[0] // 512, widen)
    lane = lax.broadcasted_iota(jnp.int32, (CH, cols), 1)
    ones = jnp.ones((8, cols), F32)

    def turn(i, carry):
        for k in range(4):
            carry = turn_row(4 * i + k, *carry)
        return carry

    def turn_row(r, west, east):
        t = jnp.concatenate([fh[pl.ds(r, CH - 8, stride=rows), :], ones], axis=0)
        slab[r + 1, CH : 2 * CH, :] = t.astype(BF16)
        west = jnp.where(lane == r, jnp.broadcast_to(t[:, 0:1], (CH, cols)), west)
        east = jnp.where(lane == r, jnp.broadcast_to(t[:, cols - 1 : cols], (CH, cols)), east)
        return west, east

    zero = jnp.zeros((CH, cols), F32)
    west, east = lax.fori_loop(0, rows // 4, turn, (zero, zero))
    cols_out[0] = west.astype(BF16)
    cols_out[1] = east.astype(BF16)

    def rim(slot, src, dst, la, lo):
        return pltpu.make_async_remote_copy(
            src_ref=src, dst_ref=dst, send_sem=sh.at[slot], recv_sem=vh.at[slot],
            device_id=(la, lo), device_id_type=MESH,
        )

    to_south = [
        rim(0, slab.at[rows, pl.ds(CH, CH)], halo.at[0], south, b),
        rim(1, cols_out.at[1], cols_in.at[0, 0], south, right),
        rim(2, cols_out.at[0], cols_in.at[1, 0], south, left),
    ]
    to_north = [
        rim(3, slab.at[1, pl.ds(CH, CH)], halo.at[1], north, b),
        rim(4, cols_out.at[1], cols_in.at[0, 2], north, right),
        rim(5, cols_out.at[0], cols_in.at[1, 2], north, left),
    ]
    level = [
        rim(6, cols_out.at[1], cols_in.at[0, 1], a, right),
        rim(7, cols_out.at[0], cols_in.at[1, 1], a, left),
    ]
    for copy in level:
        copy.start()

    @pl.when(a < lats - 1)
    def _():
        for copy in to_south:
            copy.start()

    @pl.when(a > 0)
    def _():
        for copy in to_north:
            copy.start()

    load_trig.wait()
    loop(1, lons, lambda i: first(i).wait())
    lat_weight = weights_ref[pl.ds(group // packs, 1), :]
    circles = jnp.concatenate([r1[x] for x in range(lons)], axis=1)

    def member_block(ref, member):
        return ref.at[pl.ds(pl.multiple_of(member * block, block), block)]

    def zonal(member):
        at = pl.ds(pl.multiple_of(member * block, block), block)
        total = lax.dot_general(
            trig[at, :], circles, (((1,), (1,)), ((), ())), preferred_element_type=F32
        )
        return (total * lat_weight).astype(BF16)

    def second(i):
        peer = lax.rem(group + i, members)
        return pltpu.make_async_remote_copy(
            src_ref=member_block(fsend, peer), dst_ref=member_block(r2, group),
            send_sem=s2.at[i], recv_sem=v2.at[i],
            device_id=member_device(peer), device_id_type=MESH,
        )

    def zonal_send(i):
        peer = lax.rem(group + i, members)
        member_block(fsend, peer)[...] = zonal(peer)
        second(i).start()

    loop(1, members, zonal_send)
    member_block(r2, group)[...] = zonal(group)

    wide = 9 * CH
    spot = lax.broadcasted_iota(jnp.int32, (1, wide), 1)
    tap = spot // CH
    within = spot - tap * CH
    source = jnp.where(within < CH - 8, tap * (CH - 8) + within, -1)
    pick = lax.broadcasted_iota(jnp.int32, (gw_ref.shape[0], wide), 0) == source
    spread = lax.dot_general(
        gw_ref[...], jnp.where(pick, 1.0, 0.0).astype(BF16), (((0,), (0,)), ((), ())),
        preferred_element_type=F32,
    )
    bias = jnp.transpose(jnp.broadcast_to(bias_ref[...], (128, 256)))[:, 0:1]
    high = bias.astype(BF16).astype(F32)
    middle = (bias - high).astype(BF16).astype(F32)
    low = bias - high - middle
    base = 4 * CH + CH - 8
    spread += jnp.where(spot == base, high, 0.0)
    spread += jnp.where(spot == base + 1, middle, 0.0)
    spread += jnp.where(spot == base + 2, low, 0.0)
    gate_row = lax.broadcasted_iota(jnp.int32, (256, 1), 0) // 64
    gate_w[...] = (spread * jnp.where(gate_row == 2, 1.0, 0.5)).astype(BF16)

    for copy in level:
        copy.wait()

    @pl.when(a < lats - 1)
    def _():
        for copy in to_south:
            copy.wait_send()
        for copy in to_north:
            copy.wait_recv()

    @pl.when(a > 0)
    def _():
        for copy in to_north:
            copy.wait_send()
        for copy in to_south:
            copy.wait_recv()

    @pl.when(a == 0)
    def _():
        halo[0] = jnp.zeros((CH, cols), BF16)
        cols_in[0, 0] = jnp.zeros((CH, cols), BF16)
        cols_in[1, 0] = jnp.zeros((CH, cols), BF16)

    @pl.when(a == lats - 1)
    def _():
        halo[1] = jnp.zeros((CH, cols), BF16)
        cols_in[0, 2] = jnp.zeros((CH, cols), BF16)
        cols_in[1, 2] = jnp.zeros((CH, cols), BF16)

    def shifted(t, from_west, from_east, row):
        before = jnp.where(
            lane == 0, pltpu.roll(from_west, lax.rem(cols - row, cols), 1), pltpu.roll(t, 1, 1)
        )
        after = jnp.where(
            lane == cols - 1, pltpu.roll(from_east, cols - 1 - row, 1), pltpu.roll(t, cols - 1, 1)
        )
        return before.astype(BF16), after.astype(BF16)

    def keep(at, sides):
        slab[at, 0:CH, :] = sides[0]
        slab[at, 2 * CH : 3 * CH, :] = sides[1]

    def shift_rows(i):
        from_west, from_east = cols_in[0, 1].astype(F32), cols_in[1, 1].astype(F32)
        middle = [slab[4 * i + k + 1, CH : 2 * CH, :].astype(F32) for k in range(4)]
        sides = [shifted(middle[k], from_west, from_east, 4 * i + k) for k in range(4)]
        for k in range(4):
            keep(4 * i + k + 1, sides[k])

    loop(0, rows // 4, shift_rows)
    slab[0, CH : 2 * CH, :] = halo[0]
    slab[rows + 1, CH : 2 * CH, :] = halo[1]
    first_row, last_row = [
        shifted(halo[k].astype(F32), cols_in[0, 2 * k].astype(F32), cols_in[1, 2 * k].astype(F32), at)
        for k, at in ((0, rows - 1), (1, 0))
    ]
    keep(0, first_row)
    keep(rows + 1, last_row)

    load_leg.wait()
    loop(1, members, lambda i: second(i).wait())
    tiles = lats * rows // 128
    offsets = degree_offsets(members)
    share = len(offsets) - 1
    rates[...] = jnp.zeros_like(rates)
    rates[:, :KDEG] = relax_ref[...]
    rate_row = jnp.broadcast_to(rates[pl.ds(b // per_field, 1), :], (16, 512))
    rate_row = pltpu.roll(rate_row, lax.rem(512 - group, 512), 1)
    q_mode = lax.broadcasted_iota(jnp.int32, (16, 128), 0) // 2
    for u in range(block // 16):
        x = []
        for t in range(tiles):
            total = jnp.zeros((16, 128), F32)
            for g in range(t * packs, (t + 1) * packs):
                total += r2[g * block + 16 * u : g * block + 16 * (u + 1), :].astype(F32)
            x.append(total.astype(BF16))
        low, high = 8 * u, min(8 * (u + 1), share)
        basis = leg[offsets[low] : offsets[high], :]
        s = lax.dot_general(
            jnp.concatenate(x, axis=1), basis, (((1,), (1,)), ((), ())), preferred_element_type=F32
        )
        parts = []
        for i in range(low, high):
            rate = rate_row if i == 0 else pltpu.roll(rate_row, 512 - members * i, 1)
            if i == 0:
                rate = rate * jnp.where(group == 0, 1.0 / lon_total, 2.0 / lon_total)
            else:
                rate = rate * (2.0 / lon_total)
            for k in range(0, offsets[i + 1] - offsets[i], 128):
                at = offsets[i] - offsets[low] + k
                parts.append(
                    jnp.where(q_mode == i - low, s[:, at : at + 128] * rate[:, k : k + 128], 0.0)
                )
        nudged = jnp.concatenate(parts, axis=1).astype(BF16)
        y = jnp.dot(nudged, basis, preferred_element_type=F32).astype(BF16)
        for t in range(tiles):
            ysend[t, 16 * u : 16 * (u + 1), :] = y[:, t * 128 : (t + 1) * 128]

    def third(i):
        peer = lax.rem(group + i, members)
        return pltpu.make_async_remote_copy(
            src_ref=ysend.at[peer // packs], dst_ref=member_block(r3, group),
            send_sem=s3.at[i], recv_sem=v3.at[i],
            device_id=member_device(peer), device_id_type=MESH,
        )

    loop(1, members, lambda i: third(i).start())
    member_block(r3, group)[...] = ysend[group // packs]

    load_cell.wait()

    def pair(i):
        r = 2 * i
        patches = jnp.concatenate(
            [slab[pl.ds(r, 3)].reshape(wide, cols), slab[pl.ds(r + 1, 3)].reshape(wide, cols)], axis=1
        )
        g = jnp.tanh(jnp.dot(gate_w[...], patches, preferred_element_type=F32))
        old = jnp.concatenate(
            [cell[pl.ds(r, 64, stride=rows), :], cell[pl.ds(r + 1, 64, stride=rows), :]], axis=1
        )
        new = (0.5 * g[64:128] + 0.5) * old + (0.5 * g[0:64] + 0.5) * g[128:192]
        h = (0.5 * g[192:256] + 0.5) * jnp.tanh(new)
        cell_out[pl.ds(r, 64, stride=rows), :] = new[:, :cols]
        cell_out[pl.ds(r + 1, 64, stride=rows), :] = new[:, cols:]
        hid[pl.ds(r, 64, stride=rows), :] = h[:, :cols]
        hid[pl.ds(r + 1, 64, stride=rows), :] = h[:, cols:]
        inc = jnp.dot(ow_ref[...], h.astype(BF16), preferred_element_type=F32)
        pred[pl.ds(r, FIELDS, stride=rows), :] = inc[:, :cols]
        pred[pl.ds(r + 1, FIELDS, stride=rows), :] = inc[:, cols:]

    loop(0, rows // 4, pair)

    loop(1, members, lambda i: third(i).wait())
    turned[...] = jnp.transpose(r3[...].astype(F32)).astype(BF16)
    mine = turned[pl.ds(own_row, piece), :]

    def inverse(sector):
        at = pl.ds(pl.multiple_of(sector * cols, cols), cols)
        return jnp.dot(mine, trig[:, at], preferred_element_type=F32).astype(BF16)

    spot4 = pl.ds(pl.multiple_of(b * piece, piece), piece)

    def fourth(i):
        peer = lax.rem(b + i, lons)
        return lon_copy(i, csend.at[peer], r4.at[spot4], s4, v4)

    def inverse_send(i):
        peer = lax.rem(b + i, lons)
        csend[peer] = inverse(peer)
        fourth(i).start()

    loop(1, lons, inverse_send)
    r4[spot4, :] = inverse(b)

    loop(rows // 4, rows // 2, pair)

    def narrow(c):
        at = pl.ds(pl.multiple_of(c * 512, 512), 512)
        hidden_out[at, :] = hid[at, :].astype(BF16)

    loop(0, hidden_ref.shape[0] // 512, narrow)
    loop(1, lons, lambda i: fourth(i).wait())
    fields_out[...] = (
        fields_ref[...].astype(F32) + pred[...] + r4[...].astype(F32)
    ).astype(BF16)


def local(lats, lons, leg, trig, fields_in, hidden, cell_state, analysis, gate_weight, gate_bias, out_weight, relax_rates):
    hid, rows, cols = cell_state.shape
    lat_total = lats * rows
    piece = FIELDS * rows // lons
    members = lats * rows // piece
    quads = members * block_rows(members)
    phi = -0.5 * np.pi + (np.arange(lat_total) + 0.5) * np.pi / lat_total
    weights = (np.cos(phi) * np.pi / lat_total).astype(np.float32).reshape(-1, 128)
    vm = pl.BlockSpec(memory_space=pltpu.VMEM)
    hbm = pl.BlockSpec(memory_space=pl.ANY)
    n_rows = FIELDS * rows
    dma = pltpu.SemaphoreType.DMA
    out = pl.pallas_call(
        functools.partial(kernel, lats, lons, rows, cols),
        out_shape=(
            jax.ShapeDtypeStruct((n_rows, cols), BF16),
            jax.ShapeDtypeStruct((hid * rows, cols), BF16),
            jax.ShapeDtypeStruct((hid * rows, cols), F32),
        ),
        in_specs=[vm, vm, hbm, vm, vm, vm, vm, vm, vm, hbm, hbm],
        out_specs=(vm, vm, vm),
        scratch_shapes=[
            pltpu.VMEM((n_rows, cols), BF16),
            pltpu.VMEM((lons, 128, cols), BF16),
            pltpu.VMEM(((hid + FIELDS) * rows, cols), F32),
            pltpu.VMEM((rows + 2, 3 * CH, cols), BF16),
            pltpu.VMEM((2, CH, cols), BF16),
            pltpu.VMEM((2, CH, cols), BF16),
            pltpu.VMEM((2, 3, CH, cols), BF16),
            pltpu.VMEM((quads, 128), BF16),
            pltpu.VMEM((quads, 128), BF16),
            pltpu.VMEM((lat_total // 128, quads // members, 128), BF16),
            pltpu.VMEM((quads, 128), BF16),
            pltpu.VMEM((128, quads), BF16),
            pltpu.VMEM((lons, piece, cols), BF16),
            pltpu.VMEM((n_rows, cols), BF16),
            pltpu.VMEM((FIELDS, 512), F32),
            pltpu.VMEM((4 * hid, 9 * CH), BF16),
            pltpu.VMEM((n_rows, cols), F32),
            pltpu.VMEM((hid * rows, cols), F32),
            pltpu.VMEM(trig.shape, BF16),
            pltpu.VMEM(leg.shape[1:], BF16),
            pltpu.VMEM((hid * rows, cols), F32),
            dma((3,)),
            dma((lons,)), dma((lons,)), dma((members,)), dma((members,)),
            dma((members,)), dma((members,)), dma((lons,)), dma((lons,)),
            dma((8,)), dma((8,)),
        ],
        compiler_params=pltpu.CompilerParams(
            collective_id=0, has_side_effects=True, vmem_limit_bytes=56 * 1024 * 1024
        ),
    )(
        fields_in.reshape(n_rows, cols), hidden.reshape(hid * rows, cols),
        cell_state.reshape(hid * rows, cols), analysis.reshape(n_rows, cols),
        gate_weight.T, gate_bias.reshape(1, -1), out_weight, relax_rates, jnp.asarray(weights),
        jnp.asarray(trig), jnp.asarray(leg),
    )
    return (
        out[0].reshape(fields_in.shape), out[1].reshape(hidden.shape), out[2].reshape(cell_state.shape)
    )


def solution(mesh):
    lats, lons = mesh.shape["lat"], mesh.shape["lon"]

    def whole(*args):
        lat_total, lon_total = args[2].shape[1:]
        piece = FIELDS * (lat_total // lats) // lons
        leg = legendre_table(lat_total, lat_total // piece)
        trig = trig_table(lon_total, lat_total // piece)
        grid = P(None, "lat", "lon")
        return jax.shard_map(
            functools.partial(local, lats, lons, leg, trig),
            mesh=mesh,
            in_specs=(grid, grid, grid, grid, P(), P(), P(), P()),
            out_specs=(grid, grid, grid),
            check_vma=False,
        )(*args)

    return whole
```

time: 58.2 us -> 45.6 us (0.78)
  Pallas kernels: 48.8 us -> 39.4 us
  local copies, waits for them, and re-layouts: 8.5 us -> 5.3 us
    pallas_call x1, Pallas kernels: 48.8 us -> 39.4 us  [local(): pl.pallas_call(functools.partial(kernel, lats, lons, rows, cols), out_sha...]
    unnamed x6 -> x5, local copies, waits for them, and re-layouts: 7.19 us -> 5.3 us
    pad x1 -> x0, local copies, waits for them, and re-layouts: 1.31 us -> none  [local(): relax = jnp.pad(relax_rates, ((0, 0), (0, 512 - KDEG)))]
where the time goes in v1:
time: 45.6 us; the launch traced here: 45.4 us
  Pallas kernels  39.4 us (86%)
  local copies, waits for them, and re-layouts  5.3 us (12%)
  between operations  0.65 us (1%)
    pallas_call x1, Pallas kernels, local(): pl.pallas_call(functools.partial(kernel, lats, lons, rows, cols), out_sha...  39.4 us
    unnamed x5, local copies, waits for them, and re-layouts  5.3 us

profile of v1, /device:TPU:0, one launch (start us, length us, event | category | flops | bytes accessed | tf_op | source)
XLA Modules:
  0.0 45.4 jit_solution(7992621037692817939)
XLA Ops:
  0.6 39.4 %shard_map.130 = (bf16[512,128]{1,0:T(8,128)(2,1)}, bf16[4096,128]{1,0:T(8,128)(2,1)}, f32[4096,128]{1,0:T(8,128)}) custom-call(bf16[512,128]{1,0:T(8,128)(2,1)} %bitcast.14, bf16[4096,128]{1,0:T(8,128)(2,1)} %bitcast.12, f32[4096,128]{1,0:T(8,128)} %bitcast.10, bf16[512,128]{1,0:T(8,128)(2,1)} %bitcast.15, bf16[648,256]{1,0:T(8,128)(2,1)} %bitcast.13, ...), custom_call_target="tpu_custom_call" | custom-call | tf_op jit(solution)/shard_map/pallas_call | solution.py:441
  40.1 0.0 copy-start
  40.1 1.7 %copy.17 = bf16[8,64,128]{2,1,0:T(8,128)(2,1)} copy(bf16[8,64,128]{2,1,0:T(8,128)(2,1)} %bitcast.16) | data formatting | bytes 262144
  41.8 2.3 %copy.18 = bf16[64,64,128]{2,1,0:T(8,128)(2,1)} copy(bf16[64,64,128]{2,1,0:T(8,128)(2,1)} %bitcast.11) | data formatting | bytes 2097152
  44.1 0.0 copy-done
  44.1 1.3 %copy.19 = f32[64,64,128]{2,1,0:T(8,128)} copy(f32[64,64,128]{2,1,0:T(8,128)S(1)} %bitcast.9) | data formatting | bytes 4194304
Async XLA Ops:
  40.1 4.0 %copy-start = (f32[4096,128]{1,0:T(8,128)S(1)}, f32[4096,128]{1,0:T(8,128)}, u32[]{:S(2)}) copy-start(f32[4096,128]{1,0:T(8,128)} %get-tuple-element.8) | copy-start | bytes 6291460

commit v2 on v1

--- a/solution.py
+++ b/solution.py
@@ -78,11 +78,12 @@
 
 def kernel(
     lats, lons, rows, cols,
-    fields_ref, hidden_ref, cell_ref, analysis_ref, gw_ref, bias_ref, ow_ref, relax_ref,
-    weights_ref, trig_hbm, leg_hbm,
+    fields_hbm, hidden_hbm, cell_hbm, analysis_hbm, gw_hbm, bias_hbm, ow_hbm, relax_hbm,
+    weights_hbm, trig_hbm, leg_hbm,
     fields_out, hidden_out, cell_out,
     send1, r1, fh, slab, cols_out, halo, cols_in, fsend, r2, ysend, r3, turned, csend, r4, rates,
     gate_w, pred, hid, trig, leg, cell,
+    fields_ref, hidden_ref, analysis_ref, gw_ref, bias_ref, ow_ref, relax_ref, weights_ref,
     load_sem, s1, v1, s2, v2, s3, v3, s4, v4, sh, vh,
 ):
     a, b = lax.axis_index("lat"), lax.axis_index("lon")
@@ -95,12 +96,20 @@
     own_row = pl.multiple_of(lax.rem(group, packs) * piece, piece)
     lon_total = lons * cols
 
-    load_trig = pltpu.make_async_copy(trig_hbm, trig, load_sem.at[0])
-    load_leg = pltpu.make_async_copy(leg_hbm.at[group], leg, load_sem.at[1])
-    load_cell = pltpu.make_async_copy(cell_ref, cell, load_sem.at[2])
-    load_trig.start()
-    load_leg.start()
-    load_cell.start()
+    def load(i, src, dst):
+        copy = pltpu.make_async_copy(src, dst, load_sem.at[i])
+        copy.start()
+        return copy
+
+    load_fields = load(0, fields_hbm, fields_ref)
+    load_analysis = load(1, analysis_hbm, analysis_ref)
+    load_hidden = load(2, hidden_hbm, hidden_ref)
+    load_trig = load(3, trig_hbm, trig)
+    load_weights = load(4, weights_hbm, weights_ref)
+    load_gates = [load(5, gw_hbm, gw_ref), load(6, bias_hbm, bias_ref), load(7, ow_hbm, ow_ref)]
+    load_relax = load(8, relax_hbm, relax_ref)
+    load_leg = load(9, leg_hbm.at[group], leg)
+    load_cell = load(10, cell_hbm, cell)
 
     r1[...] = jnp.zeros_like(r1)
     barrier = pltpu.get_barrier_semaphore()
@@ -126,6 +135,8 @@
         hello(south, left)
         hello(south, right)
 
+    load_fields.wait()
+    load_analysis.wait()
     send1[...] = (analysis_ref[...].astype(F32) - fields_ref[...].astype(F32)).astype(BF16)
     greeted = lons + members - 2
     greeted += 2 * (a > 0).astype(jnp.int32) + 2 * (a < lats - 1).astype(jnp.int32)
@@ -146,6 +157,8 @@
     r1[b, pl.ds(own_row, piece), :] = send1[pl.ds(pl.multiple_of(b * piece, piece), piece), :]
 
     fh[0 : FIELDS * rows, :] = fields_ref[...].astype(F32)
+
+    load_hidden.wait()
 
     def widen(c):
         at = pl.multiple_of(c * 512, 512)
@@ -208,6 +221,7 @@
             copy.start()
 
     load_trig.wait()
+    load_weights.wait()
     loop(1, lons, lambda i: first(i).wait())
     lat_weight = weights_ref[pl.ds(group // packs, 1), :]
     circles = jnp.concatenate([r1[x] for x in range(lons)], axis=1)
@@ -238,6 +252,8 @@
     loop(1, members, zonal_send)
     member_block(r2, group)[...] = zonal(group)
 
+    for copy in load_gates:
+        copy.wait()
     wide = 9 * CH
     spot = lax.broadcasted_iota(jnp.int32, (1, wide), 1)
     tap = spot // CH
@@ -319,6 +335,7 @@
     keep(rows + 1, last_row)
 
     load_leg.wait()
+    load_relax.wait()
     loop(1, members, lambda i: second(i).wait())
     tiles = lats * rows // 128
     offsets = degree_offsets(members)
@@ -441,11 +458,11 @@
     out = pl.pallas_call(
         functools.partial(kernel, lats, lons, rows, cols),
         out_shape=(
-            jax.ShapeDtypeStruct((n_rows, cols), BF16),
-            jax.ShapeDtypeStruct((hid * rows, cols), BF16),
-            jax.ShapeDtypeStruct((hid * rows, cols), F32),
+            pltpu.VMEM((n_rows, cols), BF16),
+            pltpu.VMEM((hid * rows, cols), BF16),
+            pltpu.VMEM((hid * rows, cols), F32),
         ),
-        in_specs=[vm, vm, hbm, vm, vm, vm, vm, vm, vm, hbm, hbm],
+        in_specs=[hbm] * 11,
         out_specs=(vm, vm, vm),
         scratch_shapes=[
             pltpu.VMEM((n_rows, cols), BF16),
@@ -469,13 +486,21 @@
             pltpu.VMEM(trig.shape, BF16),
             pltpu.VMEM(leg.shape[1:], BF16),
             pltpu.VMEM((hid * rows, cols), F32),
-            dma((3,)),
+            pltpu.VMEM((n_rows, cols), BF16),
+            pltpu.VMEM((hid * rows, cols), BF16),
+            pltpu.VMEM((n_rows, cols), BF16),
+            pltpu.VMEM(gate_weight.shape[::-1], BF16),
+            pltpu.VMEM((1, 4 * hid), F32),
+            pltpu.VMEM(out_weight.shape, BF16),
+            pltpu.VMEM(relax_rates.shape, F32),
+            pltpu.VMEM(weights.shape, F32),
+            dma((11,)),
             dma((lons,)), dma((lons,)), dma((members,)), dma((members,)),
             dma((members,)), dma((members,)), dma((lons,)), dma((lons,)),
             dma((8,)), dma((8,)),
         ],
         compiler_params=pltpu.CompilerParams(
-            collective_id=0, has_side_effects=True, vmem_limit_bytes=56 * 1024 * 1024
+            collective_id=0, has_side_effects=True, vmem_limit_bytes=60 * 1024 * 1024
         ),
     )(
         fields_in.reshape(n_rows, cols), hidden.reshape(hid * rows, cols),

time: 45.6 us -> 39.9 us (0.87)
  Pallas kernels: 39.4 us -> 36.1 us
  local copies, waits for them, and re-layouts: 5.3 us -> 2.95 us
    pallas_call x1, Pallas kernels: 39.4 us -> 36.1 us  [local(): pl.pallas_call(functools.partial(kernel, lats, lons, rows, cols), out_sha...]
    unnamed x5 -> x3, local copies, waits for them, and re-layouts: 5.3 us -> 2.95 us
where the time goes in v2:
time: 39.9 us; the launch traced here: 39.7 us
  Pallas kernels  36.1 us (90%)
  local copies, waits for them, and re-layouts  2.95 us (7%)
  between operations  0.64 us (2%)
    pallas_call x1, Pallas kernels, local(): pl.pallas_call(functools.partial(kernel, lats, lons, rows, cols), out_sha...  36.1 us
    unnamed x3, local copies, waits for them, and re-layouts  2.95 us

profile of v2, /device:TPU:0, one launch (start us, length us, event | category | flops | bytes accessed | tf_op | source)
XLA Modules:
  0.0 39.7 jit_solution(6364645534571600253)
XLA Ops:
  0.6 36.1 %shard_map.130 = (bf16[512,128]{1,0:T(8,128)(2,1)S(1)}, bf16[4096,128]{1,0:T(8,128)(2,1)S(1)}, f32[4096,128]{1,0:T(8,128)S(1)}) custom-call(bf16[512,128]{1,0:T(8,128)(2,1)} %bitcast.15, bf16[4096,128]{1,0:T(8,128)(2,1)} %bitcast.13, f32[4096,128]{1,0:T(8,128)} %bitcast.12, bf16[512,128]{1,0:T(8,128)(2,1)} %bitcast.16, bf16[648,256]{1,0:T(8,128)(2,1)} %bitcast.14, ...), custom_call_target="tpu_custom_call" | custom-call | tf_op jit(solution)/shard_map/pallas_call | solution.py:458
  36.8 0.7 %copy.17 = bf16[8,64,128]{2,1,0:T(8,128)(2,1)} copy(bf16[8,64,128]{2,1,0:T(8,128)(2,1)S(1)} %bitcast.11) | data formatting | bytes 262144
  37.4 1.0 %copy.18 = bf16[64,64,128]{2,1,0:T(8,128)(2,1)} copy(bf16[64,64,128]{2,1,0:T(8,128)(2,1)S(1)} %bitcast.10) | data formatting | bytes 2097152
  38.4 1.3 %copy.19 = f32[64,64,128]{2,1,0:T(8,128)} copy(f32[64,64,128]{2,1,0:T(8,128)S(1)} %bitcast.9) | data formatting | bytes 4194304
